TPU v7x, 32 devices: a whole 2x2x4 slice. The times are simulated.
32 devices in a mesh: node: 8 (over y, x, core), local: 4 (over z).
Axes of the slice: x: 2, y: 2, z: 4, core: 2. Of those that a mesh axis runs over, the one named last changes fastest.
Arguments:
- tokens: bfloat16 [4096, 5120], P('node', 'local'), may hold values from -6 to 6
- queries: bfloat16 [4096, 8192], P('node', 'local'), may hold values from -6 to 6
- key_weight: bfloat16 [5120, 1024], P('node', 'local'), may hold values from -0.078125 to 0.078125
- value_weight: bfloat16 [5120, 1024], P('node', 'local'), may hold values from -0.078125 to 0.078125
- query_gain: float32 [128], replicated, may hold values from 0.5 to 1.6
- key_gain: float32 [128], replicated, may hold values from 0.5 to 1.6
- segment_ids: int32 [8, 512], P('node'), may hold values from 0 to 255, never falling along the last dimension, each value on 1 to 256 neighbouring positions
- context_grad: bfloat16 [4096, 8192], P('node', 'local'), may hold values from -16 to 16
Outputs:
- context: bfloat16 [4096, 8192], P('node', 'local')
- token_grad: bfloat16 [4096, 5120], P('node', 'local')
- query_grad: bfloat16 [4096, 8192], P('node', 'local')
- key_weight_grad: float32 [5120, 1024], P('node', 'local')
- value_weight_grad: float32 [5120, 1024], P('node', 'local')
- gain_grads: float32 [2, 128], replicated
Inputs may be any that keep to these rules, and one draw needn't show every extreme that they name: `segment_ids`: within each row the numbers never fall; a document is a run of equal numbers of at most half of 512 tokens.
All inputs are finite; a program needn't handle non-finite values.
Results may differ from a plain program's by a relative error of at most 0.014.
Values may be sent and summed in bfloat16 or wider, within the bound.
A program may use at most 128 MiB of HBM per device.

v0:
```python
import jax
import jax.numpy as jnp
from jax import lax
from jax.sharding import PartitionSpec as P

EPS = 1e-06
THETA = 1000000.0


def rope_tables(segments, head_size):
    length = segments.shape[0]
    token_index = jnp.arange(length, dtype=jnp.int32)
    starts = jnp.concatenate([jnp.ones((1,), dtype=bool), segments[1:] != segments[:-1]])
    run_first = lax.cummax(jnp.where(starts, token_index, 0), axis=0)
    position = (token_index - run_first).astype(jnp.float32)
    frequency = THETA ** (-2.0 * jnp.arange(head_size // 2, dtype=jnp.float32) / head_size)
    angles = position[:, None] * frequency[None, :]
    return (jnp.cos(angles), jnp.sin(angles))


def rotate(values, cosine_table, sine_table):
    half_size = values.shape[-1] // 2
    first_half = values[..., :half_size]
    second_half = values[..., half_size:]
    cos_wide = cosine_table[:, None, :]
    sin_wide = sine_table[:, None, :]
    return jnp.concatenate(
        [
            first_half * cos_wide - second_half * sin_wide,
            second_half * cos_wide + first_half * sin_wide,
        ],
        axis=-1,
    )


def rotate_back(values, cosine_table, sine_table):
    half_size = values.shape[-1] // 2
    first_half = values[..., :half_size]
    second_half = values[..., half_size:]
    cos_wide = cosine_table[:, None, :]
    sin_wide = sine_table[:, None, :]
    return jnp.concatenate(
        [
            first_half * cos_wide + second_half * sin_wide,
            second_half * cos_wide - first_half * sin_wide,
        ],
        axis=-1,
    )


def normalize(values, gain_vector):
    inverse_rms = lax.rsqrt(jnp.mean(values * values, axis=-1, keepdims=True) + EPS)
    return (values * inverse_rms * gain_vector, inverse_rms)


def normalize_back(values, inverse_rms, gain_vector, upstream):
    weighted = gain_vector * upstream
    return inverse_rms * weighted - values * inverse_rms**3 * jnp.mean(
        values * weighted, axis=-1, keepdims=True
    )


def local(
    tokens, queries, key_weight, value_weight, query_gain, key_gain, segment_ids, context_grad
):
    head_size = query_gain.shape[0]
    kv_width = key_weight.shape[1]
    kv_local = kv_width // head_size
    q_local = queries.shape[1] // head_size
    group_size = q_local // kv_local
    seq_len = queries.shape[0]
    score_scale = head_size ** (-0.5)
    segments = segment_ids[0]
    cosine_table, sine_table = rope_tables(segments, head_size)
    gathered = lax.all_gather(tokens, "local", axis=1, tiled=True)
    stacked = jnp.concatenate([key_weight, value_weight], axis=1)
    projected = jnp.dot(
        gathered,
        lax.all_gather(stacked, "node", axis=0, tiled=True),
        preferred_element_type=jnp.float32,
    )
    key_raw = projected[:, :kv_width].reshape(seq_len, kv_local, head_size)
    value_bf = projected[:, kv_width:].astype(jnp.bfloat16).reshape(seq_len, kv_local, head_size)
    key_normed, key_scale = normalize(key_raw, key_gain)
    key_rot = rotate(key_normed, cosine_table, sine_table).astype(jnp.bfloat16)
    query_wide = queries.astype(jnp.float32).reshape(seq_len, q_local, head_size)
    query_normed, query_scale = normalize(query_wide, query_gain)
    query_rot = (
        rotate(query_normed, cosine_table, sine_table)
        .astype(jnp.bfloat16)
        .reshape(seq_len, kv_local, group_size, head_size)
    )
    grad_rows = context_grad.reshape(seq_len, kv_local, group_size, head_size)
    token_index = jnp.arange(seq_len, dtype=jnp.int32)
    block_rows = min(512, seq_len)
    value_acc = jnp.zeros((seq_len, kv_local, head_size), jnp.float32)
    key_acc = jnp.zeros((seq_len, kv_local, head_size), jnp.float32)
    allowed = (segments[0:block_rows, None] == segments[None, :block_rows]) & (
        token_index[None, :block_rows] <= token_index[0:block_rows, None]
    )
    scores = (
        jnp.einsum("qcgh,kch->cgqk", query_rot, key_rot, preferred_element_type=jnp.float32)
        * score_scale
    )
    exponent = jnp.where(allowed, jnp.exp(scores), 0.0)
    weights = exponent / jnp.sum(exponent, axis=-1, keepdims=True)
    rounded = weights.astype(jnp.bfloat16)
    contexts = jnp.einsum(
        "cgqk,kch->qcgh", rounded, value_bf, preferred_element_type=jnp.float32
    ).astype(jnp.bfloat16)
    dot_grad = jnp.einsum("qcgh,kch->cgqk", grad_rows, value_bf, preferred_element_type=jnp.float32)
    delta_row = jnp.sum(weights * dot_grad, axis=-1, keepdims=True)
    score_grad = (weights * (dot_grad - delta_row) * score_scale).astype(jnp.bfloat16)
    value_acc = value_acc.at[:block_rows].add(
        jnp.einsum("cgqk,qcgh->kch", rounded, grad_rows, preferred_element_type=jnp.float32)
    )
    key_acc = key_acc.at[:block_rows].add(
        jnp.einsum("cgqk,qcgh->kch", score_grad, query_rot, preferred_element_type=jnp.float32)
    )
    query_grads = jnp.einsum(
        "cgqk,kch->qcgh", score_grad, key_rot, preferred_element_type=jnp.float32
    )
    context = contexts.reshape(seq_len, q_local * head_size)
    query_rot_grad = query_grads.reshape(seq_len, q_local, head_size)
    value_grad = value_acc.astype(jnp.bfloat16).reshape(seq_len, kv_width)
    query_normed_grad = rotate_back(query_rot_grad, cosine_table, sine_table)
    key_normed_grad = rotate_back(key_acc, cosine_table, sine_table)
    query_grad = (
        normalize_back(query_wide, query_scale, query_gain, query_normed_grad)
        .astype(jnp.bfloat16)
        .reshape(seq_len, q_local * head_size)
    )
    key_grad = (
        normalize_back(key_raw, key_scale, key_gain, key_normed_grad)
        .astype(jnp.bfloat16)
        .reshape(seq_len, kv_width)
    )
    gain_query = jnp.sum(query_normed_grad * query_wide * query_scale, axis=(0, 1))
    gain_key = jnp.sum(key_normed_grad * key_raw * key_scale, axis=(0, 1))
    gain_query, gain_key = lax.psum((gain_query, gain_key), ("node", "local"))
    grad_stack = jnp.concatenate([key_grad, value_grad], axis=1)
    weight_grad = lax.psum_scatter(
        lax.dot_general(
            gathered, grad_stack, (((0,), (0,)), ((), ())), preferred_element_type=jnp.float32
        ),
        "node",
        scatter_dimension=0,
        tiled=True,
    )
    weight_back = lax.all_gather(stacked, "node", axis=0, tiled=True)
    summed = lax.psum_scatter(
        lax.dot_general(
            weight_back, grad_stack, (((1,), (1,)), ((), ())), preferred_element_type=jnp.float32
        ).astype(jnp.bfloat16),
        "local",
        scatter_dimension=0,
        tiled=True,
    ).astype(jnp.float32)
    token_grad = summed.T.astype(jnp.bfloat16)
    key_weight_grad = weight_grad[:, :kv_width]
    value_weight_grad = weight_grad[:, kv_width:]
    gain_grads = jnp.stack([gain_query, gain_key])
    return (context, token_grad, query_grad, key_weight_grad, value_weight_grad, gain_grads)


def solution(mesh):
    in_specs = (
        P("node", "local"),
        P("node", "local"),
        P("node", "local"),
        P("node", "local"),
        P(),
        P(),
        P("node", None),
        P("node", "local"),
    )
    out_specs = (
        P("node", "local"),
        P("node", "local"),
        P("node", "local"),
        P("node", "local"),
        P("node", "local"),
        P(),
    )
    return jax.shard_map(local, mesh=mesh, in_specs=in_specs, out_specs=out_specs, check_vma=False)
```

profile of v0, /device:TPU:0, one launch (start us, length us, event | category | flops | bytes accessed | tf_op | source)
XLA Modules:
  0.0 413.4 jit_solution(13872037341200731404)
XLA Ops:
  7.2 0.7 all-gather.5.cloned.1.call-update
  7.9 0.0 all-gather.3.cloned.1.call-start
  8.0 2.0 pad_maximum_fusion.2
  9.9 0.0 reduce-scatter.3.cloned.1.call-start
  10.0 0.5 convert_bitcast_fusion
  10.5 2.9 copy.132
  13.4 0.1 compare_reduce_fusion
  13.5 0.1 add_select_fusion
  13.6 0.3 reduce-window.9
  13.9 0.1 slice.95
  14.0 0.1 slice_reduce_fusion
  14.1 0.1 fusion.34
  14.2 1.0 multiply_cosine_fusion
  15.2 3.4 multiply_reduce_fusion.1
  18.6 0.8 multiply_multiply_fusion.2
  19.4 2.0 multiply_multiply_fusion
  21.4 1.6 subtract_convert_fusion
  23.0 1.9 copy.90
  24.8 1.9 copy.89
  26.7 2.9 copy.131
  29.6 0.9 fusion.29
  30.5 79.9 %all-gather.5.cloned.1.call-done = bf16[512,5120]{1,0:T(8,128)(2,1)} async-done(((bf16[512,1280]{1,0:T(8,128)(2,1)}), bf16[512,5120]{1,0:T(8,128)(2,1)}) %all-gather.5.cloned.1.call-update) | async-done | bytes 5242896 | tf_op jit(solution)/shard_map/all_gather | solution.py:75
  110.4 41.9 %all-gather.3.cloned.1.call-done = bf16[5120,512]{1,0:T(8,128)(2,1)} async-done(((bf16[640,512]{1,0:T(8,128)(2,1)}), bf16[5120,512]{1,0:T(8,128)(2,1)}) %all-gather.3.cloned.1.call-update) | async-done | bytes 5242896 | tf_op jit(solution)/shard_map/all_gather | solution.py:79
  152.3 6.7 %convolution_bitcast_fusion.1 = f32[512,512]{0,1:T(8,128)S(1)} fusion(bf16[5120,512]{1,0:T(8,128)(2,1)} %all-gather.3.cloned.1.call-done, bf16[512,5120]{1,0:T(8,128)(2,1)} %all-gather.5.cloned.1.call-done), kind=kOutput, calls=%fused_computation.38 | convolution fusion | flops 2684354560 | bytes 11534336 | tf_op jit(solution)/shard_map/dot_general | solution.py:77
  159.1 0.9 slice.107
  160.0 0.1 multiply_reduce_fusion.3
  160.1 0.1 copy-done.4
  160.2 1.2 copy.88
  161.5 0.2 multiply_multiply_fusion.1
  161.7 0.2 subtract_convert_fusion.1
  162.0 8.1 %fusion.52 = f32[2,512,512,8]{2,1,3,0:T(8,128)} fusion(bf16[512,2,128,1]{0,2,3,1:T(8,128)(2,1)S(1)} %bitcast.190, bf16[512,2,8,128]{0,3,2,1:T(8,128)(2,1)S(1)} %bitcast.180), kind=kOutput, calls=%fused_computation.97 | convolution fusion | flops 1073741824 | bytes 19136512 | tf_op jit(solution)/shard_map/qcgh,kch->cgqk/dot_general | solution.py:111
  170.1 5.3 %fusion.5 = (f32[2,8,512]{2,1,0:T(8,128)S(1)}, f32[2,512,512,8]{2,1,3,0:T(8,128)S(1)}) fusion(pred[512,512]{0,1:T(8,128)(4,1)S(1)} %copy-done.12, bf16[512,2,8,64]{3,0,2,1:T(8,128)(2,1)S(1)} %bitcast.184, bf16[512,2,8,64]{3,0,2,1:T(8,128)(2,1)S(1)} %bitcast.186, bf16[512,2,64]{2,0,1:T(8,128)(2,1)S(1)} %get-tuple-element.91, ...), kind=kOutput, calls=%fused_computation.8 | convolution fusion | flops 1091035136 | bytes 19431424 | tf_op jit(solution)/shard_map/qcgh,kch->cgqk/dot_general | solution.py:102
  175.4 5.7 %copy-done.21 = f32[2,512,512,8]{2,1,3,0:T(8,128)} copy-done((f32[2,512,512,8]{2,1,3,0:T(8,128)}, f32[2,512,512,8]{2,1,3,0:T(8,128)S(1)}, u32[]{:S(2)}) %copy-start.21) | copy-done | bytes 16777240
  181.1 4.9 %fusion.26 = bf16[2,512,128]{1,2,0:T(8,128)(2,1)} fusion(bf16[512,2,8,128]{0,3,2,1:T(8,128)(2,1)S(1)} %bitcast.181, f32[2,512,512,8]{2,1,3,0:T(8,128)S(1)} %get-tuple-element.99, f32[2,8,512]{2,1,0:T(8,128)S(1)} %get-tuple-element.98, pred[512,512]{0,1:T(8,128)(4,1)S(1)} %copy-done.12), kind=kOutput, calls=%fused_computation.41 | convolution fusion | flops 1090650112 | bytes 19431424 | tf_op jit(solution)/shard_map/cgqk,qcgh->kch/dot_general | solution.py:115
  186.1 25.9 %fusion.22 = f32[512,2,128]{2,0,1:T(8,128)} fusion(f32[2,512,512,8]{2,1,3,0:T(8,128)} %fusion.52, bf16[512,2,8,64]{3,0,2,1:T(8,128)(2,1)} %bitcast.183, bf16[512,2,8,64]{3,0,2,1:T(8,128)(2,1)} %bitcast.185, f32[2,512,512,8]{2,1,3,0:T(8,128)} %copy-done.21, f32[2,8,512]{2,1,0:T(8,128)S(1)} %get-tuple-element.98, pred[512,512]{0,1:T(8,128)(4,1)} %fusion.29), kind=kOutput, calls=%fused_computation.39 | convolution fusion | flops 1124082176 | bytes 36470784 | tf_op jit(solution)/shard_map/cgqk,qcgh->kch/dot_general | solution.py:118
  212.0 1.5 multiply_add_fusion.1
  213.5 1.1 multiply_reduce_fusion.2
  214.6 1.2 copy.98
  215.8 0.2 fusion.32
  216.0 7.8 %convolution_convert_fusion = bf16[5120,512]{1,0:T(8,128)(2,1)} fusion(bf16[5120,512]{1,0:T(8,128)(2,1)} %all-gather.3.cloned.1.call-done, bf16[512,256]{0,1:T(8,128)(2,1)} %bitcast.192, bf16[512,256]{0,1:T(8,128)(2,1)S(1)} %get-tuple-element.85), kind=kOutput, calls=%fused_computation.10 | convolution fusion | flops 2688024576 | bytes 11010048 | tf_op jit(solution)/shard_map/dot_general | solution.py:152
  223.8 0.0 reduce-scatter.5.cloned.1.call-start
  223.9 0.9 copy-done.11
  224.7 8.7 %convolution_bitcast_fusion = f32[5120,512]{0,1:T(8,128)} fusion(bf16[512,5120]{1,0:T(8,128)(2,1)} %all-gather.5.cloned.1.call-done, bf16[512,256]{0,1:T(8,128)(2,1)S(1)} %bitcast.193, bf16[512,256]{0,1:T(8,128)(2,1)S(1)} %get-tuple-element.85), kind=kOutput, calls=%fused_computation.9 | convolution fusion | flops 2685403136 | bytes 16252928 | tf_op jit(solution)/shard_map/dot_general | solution.py:143
  233.5 0.9 copy-done.13
  234.4 8.4 %fusion.19 = bf16[2,128,8,512]{3,1,2,0:T(8,128)(2,1)S(1)} fusion(bf16[512,2,128,1]{0,2,3,1:T(8,128)(2,1)S(1)} %bitcast.191, f32[2,512,512,8]{2,1,3,0:T(8,128)} %copy-done.21, f32[2,8,512]{2,1,0:T(8,128)S(1)} %get-tuple-element.98, pred[512,512]{0,1:T(8,128)(4,1)S(1)} %copy-done.13), kind=kOutput, calls=%fused_computation.37 | convolution fusion | flops 1091567616 | bytes 19431424 | tf_op jit(solution)/shard_map/cgqk,kch->qcgh/dot_general | solution.py:108
  242.8 2.4 copy.106
  245.2 25.5 %fusion.7 = f32[2,128,8,512]{3,1,2,0:T(8,128)} fusion(f32[2,512,512,8]{2,1,3,0:T(8,128)} %fusion.52, bf16[512,2,64]{2,0,1:T(8,128)(2,1)S(1)} %copy-done.17, bf16[512,2,64]{2,0,1:T(8,128)(2,1)S(1)} %copy-done.15, f32[2,512,512,8]{2,1,3,0:T(8,128)} %copy-done.21, f32[2,8,512]{2,1,0:T(8,128)S(1)} %get-tuple-element.98, pred[512,512]{0,1:T(8,128)(4,1)S(1)} %copy-done.13), kind=kOutput, calls=%fused_computation.12 | convolution fusion | flops 1120412160 | bytes 38305792 | tf_op jit(solution)/shard_map/cgqk,kch->qcgh/dot_general | solution.py:120
  270.8 4.2 %fusion.50 = (f32[512,16,64]{0,2,1:T(8,128)}, f32[512,16,64]{0,2,1:T(8,128)S(1)}) fusion(f32[512,16,128]{0,2,1:T(8,128)} %bitcast.182), kind=kLoop, calls=%fused_computation.95 | loop fusion | bytes 8388608 | tf_op jit(solution)/shard_map/slice | solution.py:39
  275.0 4.8 %copy.127 = f32[512,16,64]{2,1,0:T(8,128)} copy(f32[512,16,64]{0,2,1:T(8,128)} %get-tuple-element.82) | data formatting | bytes 4194304
  279.8 3.9 copy.126
  283.7 4.5 %multiply_add_fusion = (f32[512,16,64]{2,1,0:T(8,128)S(1)}, f32[512,16,64]{2,1,0:T(8,128)S(1)}) fusion(f32[512,16,64]{2,1,0:T(8,128)} %copy.127, f32[512,16,64]{2,1,0:T(8,128)} %copy.126, f32[512,64]{1,0:T(8,128)S(1)} %get-tuple-element.97, f32[512,64]{1,0:T(8,128)S(1)} %get-tuple-element.96), kind=kLoop, calls=%fused_computation.27 | loop fusion | flops 3145728 | bytes 8650752 | tf_op jit(solution)/shard_map/add | solution.py:44
  288.2 0.3 copy-done.1
  288.5 2.3 multiply_reduce_fusion
  290.8 1.1 mul.313
  291.9 1.1 mul.360
  293.1 1.1 mul.355
  294.2 10.3 %fusion.13 = (f32[2048]{0:T(1024)S(1)}, bf16[512,2048]{1,0:T(8,128)(2,1)}) fusion(bf16[512,2048]{1,0:T(8,128)(2,1)S(1)} %copy-done.3, f32[64,8,16,128]{3,2,1,0:T(8,128)S(1)} %bitcast.176, f32[64,8,16,128]{3,2,1,0:T(8,128)S(1)} %bitcast.177, f32[64,8,16,128]{3,2,1,0:T(8,128)S(1)} %bitcast.178, f32[64,8,16,128]{3,2,1,0:T(8,128)S(1)} %bitcast.179, ...), kind=kLoop, calls=%fused_computation.21 | loop fusion | flops 10483712 | bytes 20987904 | tf_op jit(solution)/shard_map/reduce_sum | solution.py:138
  304.6 39.6 %all-reduce = (f32[1,128]{1,0:T(1,128)S(1)}, f32[1,128]{1,0:T(1,128)S(1)}) all-reduce(f32[1,128]{1,0:T(1,128)S(1)} %bitcast.196, f32[1,128]{1,0:T(1,128)S(1)} %bitcast.195), channel_id=1, replica_groups=mesh['node'=8,'local'=4] {'node','local'}, use_global_device_ids=true, to_apply=%region_15.16 | all-reduce | flops 256 | bytes 2048 | tf_op jit(solution)/shard_map/psum | solution.py:140
  344.2 0.6 pad_maximum_fusion.9
  344.7 2.4 copy.107
  347.2 56.0 %reduce-scatter.5.cloned.1.call-done = f32[640,512]{0,1:T(8,128)} async-done(((f32[5120,512]{0,1:T(8,128)}), f32[640,512]{0,1:T(8,128)}) %reduce-scatter.5.cloned.1.call-update) | async-done | bytes 1310736 | tf_op jit(solution)/shard_map/reduce_scatter | solution.py:142
  403.2 1.4 fusion.51
  404.6 1.1 copy.108
  405.6 1.1 copy.109
  (54 shorter events, 0.3 us)
Async XLA Ops:
  7.2 2.8 copy-start.2
  7.2 103.2 %all-gather.5.cloned.1.call-start = ((), (), s32[]{:S(2)}) async-start(), calls=%async_computation.3 | async-start | bytes 6553600 | tf_op jit(solution)/shard_map/all_gather | solution.py:75
  7.9 144.4 %all-gather.3.cloned.1.call-start = ((), (), s32[]{:S(2)}) async-start(), calls=%async_computation.2 | async-start | bytes 5898240 | tf_op jit(solution)/shard_map/all_gather | solution.py:79
  9.9 334.8 %reduce-scatter.3.cloned.1.call-start = ((), (), s32[]{:S(2)}) async-start(), calls=%async_computation.4 | async-start | bytes 6553600 | tf_op jit(solution)/shard_map/reduce_scatter | solution.py:151
  10.5 2.9 copy-start.18
  13.4 6.0 %copy-start.19 = (f32[128]{0:T(128)S(1)}, f32[128]{0:T(128)}, u32[]{:S(2)}) copy-start(f32[128]{0:T(128)} %param.20) | copy-start | bytes 1540
  14.0 5.4 %copy-start = (f32[64,8,16,128]{3,2,1,0:T(8,128)S(1)}, f32[64,8,16,128]{3,2,1,0:T(8,128)}, u32[]{:S(2)}) copy-start(f32[64,8,16,128]{3,2,1,0:T(8,128)} %copy.132) | copy-start | bytes 12582916
  19.4 2.0 copy-start.6
  24.8 4.7 %copy-start.20 = (f32[128]{0:T(128)S(1)}, f32[128]{0:T(128)}, u32[]{:S(2)}) copy-start(f32[128]{0:T(128)} %param.21) | copy-start | bytes 1540
  159.1 1.1 copy-start.4
  161.9 8.1 %copy-start.14 = (bf16[512,2,64]{2,0,1:T(8,128)(2,1)}, bf16[512,2,64]{2,0,1:T(8,128)(2,1)S(1)}, u32[]{:S(2)}) copy-start(bf16[512,2,64]{2,0,1:T(8,128)(2,1)S(1)} %get-tuple-element.90) | copy-start | bytes 393220
  161.9 8.1 %copy-start.16 = (bf16[512,2,64]{2,0,1:T(8,128)(2,1)}, bf16[512,2,64]{2,0,1:T(8,128)(2,1)S(1)}, u32[]{:S(2)}) copy-start(bf16[512,2,64]{2,0,1:T(8,128)(2,1)S(1)} %get-tuple-element.91) | copy-start | bytes 393220
  162.0 8.1 %copy-start.8 = (bf16[512,16,64]{2,0,1:T(8,128)(2,1)S(1)}, bf16[512,16,64]{2,0,1:T(8,128)(2,1)}, u32[]{:S(2)}) copy-start(bf16[512,16,64]{2,0,1:T(8,128)(2,1)} %copy.90) | copy-start | bytes 3145732
  162.0 8.1 %copy-start.9 = (bf16[512,16,64]{2,0,1:T(8,128)(2,1)S(1)}, bf16[512,16,64]{2,0,1:T(8,128)(2,1)}, u32[]{:S(2)}) copy-start(bf16[512,16,64]{2,0,1:T(8,128)(2,1)} %copy.89) | copy-start | bytes 3145732
  162.0 8.1 %copy-start.12 = (pred[512,512]{0,1:T(8,128)(4,1)S(1)}, pred[512,512]{0,1:T(8,128)(4,1)}, u32[]{:S(2)}) copy-start(pred[512,512]{0,1:T(8,128)(4,1)} %fusion.29) | copy-start | bytes 786436
  175.4 5.7 %copy-start.21 = (f32[2,512,512,8]{2,1,3,0:T(8,128)}, f32[2,512,512,8]{2,1,3,0:T(8,128)S(1)}, u32[]{:S(2)}) copy-start(f32[2,512,512,8]{2,1,3,0:T(8,128)S(1)} %get-tuple-element.99) | copy-start | bytes 50331652
  212.0 3.8 copy-start.5
  223.8 0.9 copy-start.11
  223.8 179.4 %reduce-scatter.5.cloned.1.call-start = ((), (), s32[]{:S(2)}) async-start(), calls=%async_computation.5 | async-start | bytes 11796480 | tf_op jit(solution)/shard_map/reduce_scatter | solution.py:142
  233.4 0.9 copy-start.13
  242.8 2.4 copy-start.15
  242.8 2.4 copy-start.17
  283.7 4.8 %copy-start.1 = (f32[64,8,16,128]{3,2,1,0:T(8,128)S(1)}, f32[64,8,16,128]{3,2,1,0:T(8,128)}, u32[]{:S(2)}) copy-start(f32[64,8,16,128]{3,2,1,0:T(8,128)} %copy.132) | copy-start | bytes 12582916
  288.5 2.3 copy-start.7
  290.8 2.3 copy-start.10
  291.9 2.3 copy-start.3
Sparse Core Ops, SparseCore 0:
  9.6 100.7 all-gather.4
  112.8 39.4 all-gather.2
  223.9 93.7 reduce-scatter.2
  321.1 82.0 reduce-scatter.4
where the time goes:
time: 421 us; the launch traced here: 413 us
  waiting for transfers between devices  179 us (43%)
  matrix products  101 us (24%)
  local copies, waits for them, and re-layouts  45.7 us (11%)
  blocking collectives  39.6 us (9%)
  other arithmetic  33.7 us (8%)
  between operations  14.3 us (3%)
    all_gather x1, waiting for transfers between devices, local(): gathered = lax.all_gather(tokens, 'local', axis=1, tiled=True)  79.9 us
    reduce_scatter x1, waiting for transfers between devices, local(): lax.psum_scatter(lax.dot_general(gathered, grad_stack, (((0,), (0,)), (()...  56 us
    all_gather x1, waiting for transfers between devices, local(): lax.all_gather(stacked, 'node', axis=0, tiled=True)  41.9 us
    psum x1, blocking collectives, local(): gain_query, gain_key = lax.psum((gain_query, gain_key), ('node', 'local'))  39.6 us
    unnamed x51, local copies, waits for them, and re-layouts  26.5 us
    dot_general x1, matrix products, local(): jnp.einsum('cgqk,qcgh->kch', score_grad, query_rot, preferred_element_typ...  25.9 us
    dot_general x1, matrix products, local(): jnp.einsum('cgqk,kch->qcgh', score_grad, key_rot, preferred_element_type=...  25.5 us
    reduce_sum x2, other arithmetic, local(): jnp.sum(query_normed_grad * query_wide * query_scale, axis=(0, 1))  10.3 us
  transfers between devices with their start and end apart: 4, of which 3 were waited for; matrix products, arithmetic and copies ran while one was open for 25% of the time, Pallas kernels for 0%

commit v1 on v0

v1 whole, which is shorter than its diff:
```python
import functools
import math

import jax
import jax.numpy as jnp
from jax import lax
from jax.experimental import pallas as pl
from jax.experimental.pallas import tpu as pltpu
from jax.sharding import PartitionSpec as P

EPS = 1e-06
THETA = 1000000.0
BLOCKED = -1e30


def tables(segments, head_size):
    length = segments.shape[0]
    token_index = jnp.arange(length, dtype=jnp.int32)
    starts = jnp.concatenate([jnp.ones((1,), dtype=bool), segments[1:] != segments[:-1]])
    run_first = lax.cummax(jnp.where(starts, token_index, 0), axis=0)
    position = (token_index - run_first).astype(jnp.float32)
    frequency = THETA ** (-2.0 * jnp.arange(head_size // 2, dtype=jnp.float32) / head_size)
    angles = frequency[:, None] * position[None, :]
    allowed = (segments[:, None] == segments[None, :]) & (
        token_index[:, None] <= token_index[None, :]
    )
    bias = jnp.where(allowed, 0.0, BLOCKED).astype(jnp.float32)
    return jnp.cos(angles), jnp.sin(angles), bias


def turn(values, c1, s1, c2, s2):
    half = values.shape[0] // 2
    a, b = values[:half], values[half:]
    return jnp.concatenate([a * c1 - b * s2, b * c2 + a * s1], axis=0)


def turn_back(values, c1, s1, c2, s2):
    half = values.shape[0] // 2
    a, b = values[:half], values[half:]
    return jnp.concatenate([a * c1 + b * s1, b * c2 - a * s2], axis=0)


def attention_kernel(
    heads, block, window,
    q_ref, g_ref, k_ref, v_ref, cos_ref, sin_ref, bias_ref, gain_ref,
    ctx_ref, qg_ref, kg_ref, vg_ref, gains_ref,
    qtab, kt, kn, vt, vn, dk, dv, gq, gk,
):
    c, g = pl.program_id(0), pl.program_id(1)
    last_c, last_g = pl.num_programs(0) - 1, pl.num_programs(1) - 1
    seq, head = k_ref.shape
    half = head // 2
    score_scale = head ** (-0.5)
    exp_scale = score_scale * math.log2(math.e)

    @pl.when((c == 0) & (g == 0))
    def _():
        gq[...] = jnp.zeros_like(gq)
        gk[...] = jnp.zeros_like(gk)
        cos, sin = cos_ref[...], sin_ref[...]
        for which in range(2):
            low = gain_ref[:half, which : which + 1]
            high = gain_ref[half:, which : which + 1]
            qtab[4 * which + 0] = low * cos
            qtab[4 * which + 1] = low * sin
            qtab[4 * which + 2] = high * cos
            qtab[4 * which + 3] = high * sin

    @pl.when(g == 0)
    def _():
        raw = k_ref[...].T
        scale = lax.rsqrt(jnp.mean(raw * raw, axis=0, keepdims=True) + EPS)
        rot = turn(raw, qtab[4], qtab[5], qtab[6], qtab[7]) * scale
        kt[...] = rot.astype(jnp.bfloat16)
        kn[...] = rot.T.astype(jnp.bfloat16)
        values = v_ref[...]
        vn[...] = values.astype(jnp.bfloat16)
        vt[...] = values.T.astype(jnp.bfloat16)
        dk[...] = jnp.zeros_like(dk)
        dv[...] = jnp.zeros_like(dv)

    c1, s1, c2, s2 = qtab[0], qtab[1], qtab[2], qtab[3]
    for h in range(heads):
        cols = slice(h * head, (h + 1) * head)
        q = q_ref[:, cols].astype(jnp.float32).T
        grad = g_ref[:, cols]
        grad_t = grad.astype(jnp.float32).T.astype(jnp.bfloat16)
        scale = lax.rsqrt(jnp.mean(q * q, axis=0, keepdims=True) + EPS)
        rot = turn(q, c1, s1, c2, s2) * scale
        rot_t = rot.astype(jnp.bfloat16)
        rot_n = rot.T.astype(jnp.bfloat16)
        parts = []
        for start in range(0, seq, block):
            stop = start + block
            first = max(0, (start - window + 1) // block * block)
            keys = slice(first, stop)
            rows = slice(start, stop)
            s = jnp.dot(kn[keys], rot_t[:, rows], preferred_element_type=jnp.float32)
            e = jnp.exp2(s * exp_scale + bias_ref[keys, rows])
            inv = 1.0 / jnp.sum(e, axis=0, keepdims=True)
            w = e * inv
            p = w.astype(jnp.bfloat16)
            dp = jnp.dot(vn[keys], grad_t[:, rows], preferred_element_type=jnp.float32)
            delta = jnp.sum(w * dp, axis=0, keepdims=True)
            ds = (w * (dp - delta)).astype(jnp.bfloat16)
            ctx = jnp.dot(vt[:, keys], p, preferred_element_type=jnp.float32)
            ctx_ref[rows, cols] = ctx.T.astype(jnp.bfloat16)
            parts.append(jnp.dot(kt[:, keys], ds, preferred_element_type=jnp.float32))
            dv[keys] += jnp.dot(p, grad[rows], preferred_element_type=jnp.float32)
            dk[keys] += jnp.dot(ds, rot_n[rows], preferred_element_type=jnp.float32)
        rot_grad = jnp.concatenate(parts, axis=1)
        u = turn_back(rot_grad, c1, s1, c2, s2)
        scale_u = scale * score_scale
        t = q * u
        mean = jnp.mean(t, axis=0, keepdims=True)
        gq[...] += t * scale_u
        q_grad = u * scale_u - q * (scale * scale * scale_u * mean)
        qg_ref[:, cols] = q_grad.T.astype(jnp.bfloat16)

    @pl.when(g == last_g)
    def _():
        raw = k_ref[...].T
        scale = lax.rsqrt(jnp.mean(raw * raw, axis=0, keepdims=True) + EPS)
        u = turn_back(dk[...].T, qtab[4], qtab[5], qtab[6], qtab[7])
        scale_u = scale * score_scale
        t = raw * u
        mean = jnp.mean(t, axis=0, keepdims=True)
        gk[...] += t * scale_u
        k_grad = u * scale_u - raw * (scale * scale * scale_u * mean)
        kg_ref[...] = k_grad.T.astype(jnp.bfloat16)
        vg_ref[...] = dv[...].astype(jnp.bfloat16)

    @pl.when((c == last_c) & (g == last_g))
    def _():
        gains_ref[0:1] = (jnp.sum(gq[...], axis=1, keepdims=True) / gain_ref[:, 0:1]).T
        gains_ref[1:2] = (jnp.sum(gk[...], axis=1, keepdims=True) / gain_ref[:, 1:2]).T


def attention(queries, context_grad, projected, cos, sin, bias, gains, head, block=256, heads=4):
    seq, width = queries.shape
    kv = projected.shape[1] // (2 * head)
    group = width // head // kv
    heads = math.gcd(heads, group)
    steps = group // heads
    wide = pl.BlockSpec((seq, heads * head), lambda c, g: (0, c * steps + g))
    narrow = pl.BlockSpec((seq, head), lambda c, g: (0, c))
    whole = lambda shape: pl.BlockSpec(shape, lambda c, g: (0, 0))
    f32, bf16 = jnp.float32, jnp.bfloat16
    return pl.pallas_call(
        functools.partial(attention_kernel, heads, block, seq // 2),
        grid=(kv, steps),
        in_specs=[
            wide,
            wide,
            narrow,
            pl.BlockSpec((seq, head), lambda c, g: (0, kv + c)),
            whole(cos.shape),
            whole(sin.shape),
            whole(bias.shape),
            whole(gains.shape),
        ],
        out_specs=[wide, wide, narrow, narrow, whole((2, head))],
        out_shape=[
            jax.ShapeDtypeStruct((seq, width), bf16),
            jax.ShapeDtypeStruct((seq, width), bf16),
            jax.ShapeDtypeStruct((seq, kv * head), bf16),
            jax.ShapeDtypeStruct((seq, kv * head), bf16),
            jax.ShapeDtypeStruct((2, head), f32),
        ],
        scratch_shapes=[
            pltpu.VMEM((8, head // 2, seq), f32),
            pltpu.VMEM((head, seq), bf16),
            pltpu.VMEM((seq, head), bf16),
            pltpu.VMEM((head, seq), bf16),
            pltpu.VMEM((seq, head), bf16),
            pltpu.VMEM((seq, head), f32),
            pltpu.VMEM((seq, head), f32),
            pltpu.VMEM((head, seq), f32),
            pltpu.VMEM((head, seq), f32),
        ],
        compiler_params=pltpu.CompilerParams(
            dimension_semantics=("arbitrary", "arbitrary"), vmem_limit_bytes=48 * 2**20
        ),
        cost_estimate=pl.CostEstimate(
            flops=9 * seq * seq * width, bytes_accessed=8 * seq * width, transcendentals=0
        ),
    )(queries, context_grad, projected, projected, cos, sin, bias, gains)


def local(
    tokens, queries, key_weight, value_weight, query_gain, key_gain, segment_ids, context_grad
):
    head = query_gain.shape[0]
    kv_width = key_weight.shape[1]
    cos, sin, bias = tables(segment_ids[0], head)
    gains = jnp.stack([query_gain, key_gain], axis=1)
    gathered = lax.all_gather(tokens, "local", axis=1, tiled=True)
    stacked = jnp.concatenate([key_weight, value_weight], axis=1)
    weight_all = lax.all_gather(stacked, "node", axis=0, tiled=True)
    projected = jnp.dot(gathered, weight_all, preferred_element_type=jnp.float32)
    context, query_grad, key_grad, value_grad, gain_part = attention(
        queries, context_grad, projected, cos, sin, bias, gains, head
    )
    grad_stack = jnp.concatenate([key_grad, value_grad], axis=1)
    summed = lax.psum_scatter(
        lax.dot_general(
            weight_all, grad_stack, (((1,), (1,)), ((), ())), preferred_element_type=jnp.float32
        ).astype(jnp.bfloat16),
        "local",
        scatter_dimension=0,
        tiled=True,
    )
    token_grad = summed.T
    weight_grad = lax.psum_scatter(
        lax.dot_general(
            gathered, grad_stack, (((0,), (0,)), ((), ())), preferred_element_type=jnp.float32
        ).astype(jnp.bfloat16),
        "node",
        scatter_dimension=0,
        tiled=True,
    ).astype(jnp.float32)
    gain_grads = lax.psum(gain_part, ("node", "local"))
    key_weight_grad = weight_grad[:, :kv_width]
    value_weight_grad = weight_grad[:, kv_width:]
    return (context, token_grad, query_grad, key_weight_grad, value_weight_grad, gain_grads)


def solution(mesh):
    spread = P("node", "local")
    in_specs = (spread, spread, spread, spread, P(), P(), P("node", None), spread)
    out_specs = (spread, spread, spread, spread, spread, P())
    return jax.shard_map(local, mesh=mesh, in_specs=in_specs, out_specs=out_specs, check_vma=False)
```

time: 421 us -> 355 us (0.84); the launches traced: 413 us -> 355 us
  matrix products: 101 us -> 18.4 us
  waiting for transfers between devices: 179 us -> 242 us
  local copies, waits for them, and re-layouts: 45.7 us -> 14.3 us
  other arithmetic: 33.7 us -> 5.46 us
  Pallas kernels: 0 us -> 21.3 us
    dot_general x8 -> x2, matrix products: 92.7 us -> 13.6 us  [the longest x1 7.16 us: local(): lax.dot_general(weight_all, grad_stack, (((1,), (1,)), ((), ())), preferr...]
    reduce_scatter x2 -> x1, waiting for transfers between devices: 56 us -> 92.4 us  [local(): lax.psum_scatter(lax.dot_general(weight_all, grad_stack, (((1,), (1,)), (...]
    pallas_call x0 -> x1, Pallas kernels: none -> 21.3 us  [attention(): pl.pallas_call(functools.partial(attention_kernel, heads, block, seq // 2...]
    reduce_sum x8 -> x0, other arithmetic: 17.3 us -> none  [the longest x2 10.3 us: local(): jnp.sum(query_normed_grad * query_wide * query_scale, axis=(0, 1))]
    all_gather x1, waiting for transfers between devices: 79.9 us -> 96.6 us  [local(): gathered = lax.all_gather(tokens, 'local', axis=1, tiled=True)]
    unnamed x51 -> x10, local copies, waits for them, and re-layouts: 26.5 us -> 13.9 us
    unnamed x4 -> x5, waiting for transfers between devices: 0.73 us -> 11 us
    add x2 -> x0, other arithmetic: 5.96 us -> none  [rotate_back(): first_half * cos_wide + second_half * sin_wide]
  transfers between devices with their start and end apart: 4 -> 4, of which waited for: 3 -> 4; matrix products, arithmetic and copies ran while one was open for 25% -> 5% of each run, Pallas kernels for 0% -> 0%
where the time goes in v1:
time: 355 us
  waiting for transfers between devices  242 us (68%)
  blocking collectives  39.3 us (11%)
  Pallas kernels  21.3 us (6%)
  matrix products  18.4 us (5%)
  local copies, waits for them, and re-layouts  14.3 us (4%)
  between operations  13.8 us (4%)
  other arithmetic  5.46 us (2%)
    all_gather x1, waiting for transfers between devices, local(): gathered = lax.all_gather(tokens, 'local', axis=1, tiled=True)  96.6 us
    reduce_scatter x1, waiting for transfers between devices, local(): lax.psum_scatter(lax.dot_general(weight_all, grad_stack, (((1,), (1,)), (...  92.4 us
    all_gather x1, waiting for transfers between devices, local(): weight_all = lax.all_gather(stacked, 'node', axis=0, tiled=True)  41.9 us
    psum x1, blocking collectives, local(): gain_grads = lax.psum(gain_part, ('node', 'local'))  39.3 us
    pallas_call x1, Pallas kernels, attention(): pl.pallas_call(functools.partial(attention_kernel, heads, block, seq // 2...  21.3 us
    unnamed x10, local copies, waits for them, and re-layouts  13.9 us
    unnamed x5, waiting for transfers between devices  11 us
    dot_general x1, matrix products, local(): lax.dot_general(weight_all, grad_stack, (((1,), (1,)), ((), ())), preferr...  7.16 us
  transfers between devices with their start and end apart: 4, of which 4 were waited for; matrix products, arithmetic and copies ran while one was open for 5% of the time, Pallas kernels for 0%

profile of v1, /device:TPU:0, one launch (start us, length us, event | category | flops | bytes accessed | tf_op | source)
XLA Modules:
  0.0 354.7 jit_solution(10702925123031456021)
XLA Ops:
  7.2 0.0 all-gather.5.cloned.1.call-start
  7.2 0.7 all-gather.5.cloned.1.call-update
  7.9 0.0 all-gather.3.cloned.1.call-start
  7.9 2.0 pad_maximum_fusion
  9.9 0.0 all-gather.3.cloned.1.call-update
  9.9 0.0 reduce-scatter.7.cloned.1.call-start
  10.0 0.8 compare_reduce_fusion
  10.8 0.1 add_select_fusion
  10.9 0.3 reduce-window.9
  11.2 0.1 slice.23
  11.3 0.7 pad_maximum_fusion.1
  12.0 0.1 copy.27.gain_ref
  12.1 0.1 slice_reduce_fusion
  12.2 0.1 fusion.3
  12.3 0.5 multiply_sine_fusion
  12.9 0.9 fusion.2.bias_ref
  13.8 0.0 copy-start
  13.8 96.6 %all-gather.5.cloned.1.call-done = bf16[512,5120]{1,0:T(8,128)(2,1)} async-done(((bf16[512,1280]{1,0:T(8,128)(2,1)}), bf16[512,5120]{1,0:T(8,128)(2,1)}) %all-gather.5.cloned.1.call-update) | async-done | bytes 5242896 | tf_op jit(solution)/shard_map/all_gather | solution.py:197
  110.4 41.9 %all-gather.3.cloned.1.call-done = bf16[5120,512]{1,0:T(8,128)(2,1)} async-done(((bf16[640,512]{1,0:T(8,128)(2,1)}), bf16[5120,512]{1,0:T(8,128)(2,1)}) %all-gather.3.cloned.1.call-update) | async-done | bytes 5242896 | tf_op jit(solution)/shard_map/all_gather | solution.py:199
  152.4 6.5 %convolution_bitcast_fusion.k_ref.v_ref = f32[512,512]{1,0:T(8,128)S(1)} fusion(bf16[512,5120]{1,0:T(8,128)(2,1)} %all-gather.5.cloned.1.call-done, bf16[5120,512]{1,0:T(8,128)(2,1)} %all-gather.3.cloned.1.call-done), kind=kOutput, calls=%fused_computation.3 | convolution fusion | flops 2684354560 | bytes 11534336 | tf_op jit(solution)/shard_map/dot_general | solution.py:200
  158.8 0.0 copy-done
  158.8 0.0 copy-start.1
  158.8 21.3 %shard_map.127 = (bf16[512,2048]{1,0:T(8,128)(2,1)}, bf16[512,2048]{1,0:T(8,128)(2,1)}, bf16[512,256]{1,0:T(8,128)(2,1)S(1)}, bf16[512,256]{1,0:T(8,128)(2,1)S(1)}, f32[2,128]{1,0:T(2,128)S(1)}) custom-call(bf16[512,2048]{1,0:T(8,128)(2,1)S(1)} %copy-done, bf16[512,2048]{1,0:T(8,128)(2,1)} %g_ref.1, f32[512,512]{1,0:T(8,128)S(1)} %convolution_bitcast_fusion.k_ref.v_ref, ...), custom_call_target="tpu_custom_call" | custom-call | flops 4831838208 | bytes 8388608 | tf_op jit(solution)/shard_map/pallas_call | solution.py:149
  180.2 0.0 copy-done.1
  180.2 4.8 %fusion = bf16[5120,512]{0,1:T(8,128)(2,1)} fusion(bf16[512,512]{1,0:T(8,128)(2,1)S(1)} %constant_dynamic-update-slice_fusion, bf16[512,5120]{1,0:T(8,128)(2,1)S(1)} %copy-done.1), kind=kOutput, calls=%fused_computation.2 | convolution fusion | flops 2686976000 | bytes 11010048 | tf_op jit(solution)/shard_map/dot_general | solution.py:215
  185.0 7.9 %copy.32 = bf16[5120,512]{1,0:T(8,128)(2,1)} copy(bf16[5120,512]{0,1:T(8,128)(2,1)} %fusion) | data formatting | bytes 10485760
  192.9 0.0 reduce-scatter.7.cloned.1.call-update
  192.9 0.0 reduce-scatter.5.cloned.1.call-start
  193.0 7.2 %convolution_convert_fusion.1 = bf16[5120,512]{1,0:T(8,128)(2,1)} fusion(bf16[5120,512]{1,0:T(8,128)(2,1)} %all-gather.3.cloned.1.call-done, bf16[512,512]{1,0:T(8,128)(2,1)S(1)} %constant_dynamic-update-slice_fusion), kind=kOutput, calls=%fused_computation.1 | convolution fusion | flops 2686976000 | bytes 11010048 | tf_op jit(solution)/shard_map/dot_general | solution.py:206
  200.1 0.0 reduce-scatter.5.cloned.1.call-update
  200.2 39.3 %psum.7 = f32[2,128]{1,0:T(2,128)} all-reduce(f32[2,128]{1,0:T(2,128)S(1)} %get-tuple-element.15), channel_id=1, replica_groups=mesh['node'=8,'local'=4] {'node','local'}, use_global_device_ids=true, to_apply=%region_4.5 | all-reduce | flops 256 | bytes 2048 | tf_op jit(solution)/shard_map/psum | solution.py:222
  239.5 10.2 %reduce-scatter.7.cloned.1.call-done = bf16[640,512]{1,0:T(8,128)(2,1)} async-done(((bf16[5120,512]{1,0:T(8,128)(2,1)}), bf16[640,512]{1,0:T(8,128)(2,1)}) %reduce-scatter.7.cloned.1.call-update) | async-done | bytes 655376
  249.7 1.4 copy.33
  251.1 0.1 fusion.4
  251.2 1.1 copy.30
  252.3 1.1 copy.29
  253.4 92.4 %reduce-scatter.5.cloned.1.call-done = bf16[1280,512]{1,0:T(8,128)(2,1)} async-done(((bf16[5120,512]{1,0:T(8,128)(2,1)}), bf16[1280,512]{1,0:T(8,128)(2,1)}) %reduce-scatter.5.cloned.1.call-update) | async-done | bytes 1310736 | tf_op jit(solution)/shard_map/reduce_scatter | solution.py:205
  345.8 2.4 copy.28
  (4 shorter events, 0.1 us)
Async XLA Ops:
  7.2 103.2 %all-gather.5.cloned.1.call-start = ((), (), s32[]{:S(2)}) async-start(), calls=%async_computation.3 | async-start | bytes 6553600 | tf_op jit(solution)/shard_map/all_gather | solution.py:197
  7.9 144.4 %all-gather.3.cloned.1.call-start = ((), (), s32[]{:S(2)}) async-start(), calls=%async_computation.2 | async-start | bytes 5898240 | tf_op jit(solution)/shard_map/all_gather | solution.py:199
  9.9 239.8 %reduce-scatter.7.cloned.1.call-start = ((), (), s32[]{:S(2)}) async-start(), calls=%async_computation.5 | async-start | bytes 5898240
  13.8 145.0 %copy-start = (bf16[512,2048]{1,0:T(8,128)(2,1)S(1)}, bf16[512,2048]{1,0:T(8,128)(2,1)}, u32[]{:S(2)}) copy-start(bf16[512,2048]{1,0:T(8,128)(2,1)} %q_ref.1) | copy-start | bytes 6291460
  158.8 21.4 %copy-start.1 = (bf16[512,5120]{1,0:T(8,128)(2,1)S(1)}, bf16[512,5120]{1,0:T(8,128)(2,1)}, u32[]{:S(2)}) copy-start(bf16[512,5120]{1,0:T(8,128)(2,1)} %all-gather.5.cloned.1.call-done) | copy-start | bytes 15728644
  192.9 152.9 %reduce-scatter.5.cloned.1.call-start = ((), (), s32[]{:S(2)}) async-start(), calls=%async_computation.4 | async-start | bytes 6553600 | tf_op jit(solution)/shard_map/reduce_scatter | solution.py:205
Sparse Core Ops, SparseCore 0:
  9.6 100.7 all-gather.4
  112.9 39.4 all-gather.2
  193.0 56.6 reduce-scatter.6
  252.0 93.7 reduce-scatter.4

commit v2 on v1

--- a/solution.py
+++ b/solution.py
@@ -187,39 +187,375 @@
     )(queries, context_grad, projected, projected, cos, sin, bias, gains)
 
 
+def line_gather(size, me, own_ref, all_ref, send_sem, recv_sem):
+    def copy(way, step, block, source):
+        return pltpu.make_async_remote_copy(
+            src_ref=source,
+            dst_ref=all_ref.at[block],
+            send_sem=send_sem.at[way, step],
+            recv_sem=recv_sem.at[way, step],
+            device_id={"local": me + 1 if way == 0 else me - 1},
+            device_id_type=pl.DeviceIdType.MESH,
+        )
+
+    def sent(way, step):
+        block = me - step if way == 0 else me + step
+        return block, (block >= 0) & (me + 1 < size) if way == 0 else (block < size) & (me >= 1)
+
+    def begin(way, step):
+        block, there = sent(way, step)
+
+        @pl.when(there)
+        def _():
+            copy(way, step, block, own_ref if step == 0 else all_ref.at[block]).start()
+
+    def arrive(step):
+        for way in range(2):
+            block = me - 1 - step if way == 0 else me + 1 + step
+
+            @pl.when(block >= 0 if way == 0 else block < size)
+            def _():
+                copy(way, step, block, own_ref).wait_recv()
+
+            if step + 1 < size - 1:
+                begin(way, step + 1)
+
+    def finish():
+        for step in range(size - 1):
+            for way in range(2):
+                block, there = sent(way, step)
+
+                @pl.when(there)
+                def _():
+                    copy(way, step, block, own_ref).wait_send()
+
+    def start():
+        for way in range(2):
+            begin(way, 0)
+
+    return start, arrive, finish
+
+
+def greet(nodes, locals_, node, me, all_locals, more=0):
+    barrier = pltpu.get_barrier_semaphore()
+
+    def signal(device):
+        pl.semaphore_signal(
+            barrier, inc=1, device_id=device, device_id_type=pl.DeviceIdType.MESH
+        )
+
+    for j in range(1, nodes):
+        signal({"node": lax.rem(node + j, nodes)})
+    if all_locals:
+        for j in range(1, locals_):
+            signal({"local": lax.rem(me + j, locals_)})
+        pl.semaphore_wait(barrier, nodes - 1 + locals_ - 1)
+    else:
+        for edge, to in ((me >= 1, me - 1), (me + 1 < locals_, me + 1)):
+
+            @pl.when(edge)
+            def _():
+                signal({"local": to})
+
+        near = jnp.where(me >= 1, 1, 0) + jnp.where(me + 1 < locals_, 1, 0)
+        pl.semaphore_wait(barrier, nodes - 1 + near + more)
+
+
+def exchange(axis, size, me, slots, send_sem, recv_sem):
+    def copy(j, slot):
+        return pltpu.make_async_remote_copy(
+            src_ref=slots.at[slot],
+            dst_ref=slots.at[slot],
+            send_sem=send_sem.at[j - 1],
+            recv_sem=recv_sem.at[j - 1],
+            device_id={axis: lax.rem(me + j, size)},
+            device_id_type=pl.DeviceIdType.MESH,
+        )
+
+    def start():
+        for j in range(1, size):
+            copy(j, me).start()
+
+    def finish():
+        for j in range(1, size):
+            copy(j, lax.rem(me + size - j, size)).wait_recv()
+        for j in range(1, size):
+            copy(j, me).wait_send()
+
+    return start, finish
+
+
+def pair_exchange(size, me, slots, same_send, same_recv, cross_send, cross_recv):
+    half, parity, place = size // 2, lax.rem(me, 2), me // 2
+
+    def slot(j, side):
+        return lax.rem(place + half - j, half) * 2 + side
+
+    def same(j, which):
+        return pltpu.make_async_remote_copy(
+            src_ref=slots.at[which],
+            dst_ref=slots.at[which],
+            send_sem=same_send.at[j],
+            recv_sem=same_recv.at[j],
+            device_id={"node": lax.rem(place + j, half) * 2 + parity},
+            device_id_type=pl.DeviceIdType.MESH,
+        )
+
+    def cross(j, which):
+        return pltpu.make_async_remote_copy(
+            src_ref=slots.at[which],
+            dst_ref=slots.at[which],
+            send_sem=cross_send.at[j],
+            recv_sem=cross_recv.at[j],
+            device_id={"node": me + 1 - 2 * parity},
+            device_id_type=pl.DeviceIdType.MESH,
+        )
+
+    def start():
+        for j in range(1, half):
+            same(j, me).start()
+        cross(0, me).start()
+
+    def relay():
+        for j in range(1, half):
+            same(j, slot(j, parity)).wait_recv()
+            cross(j, slot(j, parity)).start()
+
+    def arrived():
+        for j in range(half):
+            cross(j, slot(j, 1 - parity)).wait_recv()
+
+    def finish():
+        for j in range(1, half):
+            same(j, me).wait_send()
+        for j in range(half):
+            cross(j, slot(j, parity)).wait_send()
+
+    return start, relay, arrived, finish
+
+
+def project_kernel(
+    nodes, locals_, tokens_ref, kw_ref, vw_ref, all_ref, out_ref, rows_ref,
+    slots, line_send, line_recv, col_sems, row_sems, trade_sems, own_sem,
+):
+    node, me = lax.axis_index("node"), lax.axis_index("local")
+    ratio = nodes // locals_
+    kv_width = kw_ref.shape[1]
+    seq, depth = tokens_ref.shape
+    rows = kw_ref.shape[0]
+    own = pltpu.make_async_copy(tokens_ref, all_ref.at[me], own_sem)
+    own.start()
+    slots[node, :, :kv_width] = kw_ref[...]
+    slots[node, :, kv_width:] = vw_ref[...]
+    peer_node, peer_local = me * ratio + lax.rem(node, ratio), node // ratio
+    moves = peer_local != me
+    peer = {"node": peer_node, "local": peer_local}
+
+    @pl.when(moves)
+    def _():
+        barrier = pltpu.get_barrier_semaphore()
+        pl.semaphore_signal(
+            barrier, inc=1, device_id=peer, device_id_type=pl.DeviceIdType.MESH
+        )
+
+    greet(nodes, locals_, node, me, False, jnp.where(moves, 1, 0))
+
+    def trade(slot):
+        return pltpu.make_async_remote_copy(
+            src_ref=slots.at[node],
+            dst_ref=rows_ref.at[slot],
+            send_sem=trade_sems.at[0],
+            recv_sem=trade_sems.at[1],
+            device_id=peer,
+            device_id_type=pl.DeviceIdType.MESH,
+        )
+
+    @pl.when(moves)
+    def _():
+        trade(peer_node).start()
+
+    @pl.when(jnp.logical_not(moves))
+    def _():
+        rows_ref[node, :, :kv_width] = kw_ref[...]
+        rows_ref[node, :, kv_width:] = vw_ref[...]
+
+    start, arrive, finish = line_gather(
+        locals_, me, tokens_ref, all_ref, line_send, line_recv
+    )
+    col_start, col_relay, col_arrived, col_finish = pair_exchange(
+        nodes, node, slots, *(col_sems.at[i] for i in range(4))
+    )
+    row_start, row_relay, row_arrived, row_finish = pair_exchange(
+        nodes, node, rows_ref, *(row_sems.at[i] for i in range(4))
+    )
+    start()
+    col_start()
+    out_ref[...] = jnp.zeros_like(out_ref)
+    own.wait()
+
+    def multiply(block):
+        tile = min(256, seq)
+
+        @pl.loop(0, seq // tile)
+        def _(i):
+            lines = pl.ds(pl.multiple_of(i * tile, tile), tile)
+            total = out_ref[lines, :]
+            for r in range(ratio):
+                total += jnp.dot(
+                    all_ref[block, lines, r * rows : (r + 1) * rows],
+                    slots[block * ratio + r],
+                    preferred_element_type=jnp.float32,
+                )
+            out_ref[lines, :] = total
+
+    col_relay()
+    if locals_ > 2:
+        arrive(0)
+
+    @pl.when(moves)
+    def _():
+        trade(node).wait_recv()
+
+    row_start()
+    for step in range(1, locals_ - 2):
+        arrive(step)
+    row_relay()
+    col_arrived()
+
+    @pl.loop(0, locals_)
+    def _(block):
+        @pl.when((block - me < locals_ - 1) & (me - block < locals_ - 1))
+        def _():
+            multiply(block)
+
+    arrive(locals_ - 2)
+
+    @pl.when((me == 0) | (me == locals_ - 1))
+    def _():
+        multiply(locals_ - 1 - me)
+
+    row_arrived()
+    finish()
+    col_finish()
+    row_finish()
+
+    @pl.when(moves)
+    def _():
+        trade(peer_node).wait_send()
+
+
+def project(nodes, locals_, tokens, key_weight, value_weight):
+    seq, depth = tokens.shape
+    rows, kv_width = key_weight.shape
+    vmem = pl.BlockSpec(memory_space=pltpu.VMEM)
+    return pl.pallas_call(
+        functools.partial(project_kernel, nodes, locals_),
+        in_specs=[vmem] * 3,
+        out_specs=[vmem] * 3,
+        out_shape=[
+            jax.ShapeDtypeStruct((locals_, seq, depth), jnp.bfloat16),
+            jax.ShapeDtypeStruct((seq, 2 * kv_width), jnp.float32),
+            jax.ShapeDtypeStruct((nodes, rows, 2 * kv_width), jnp.bfloat16),
+        ],
+        scratch_shapes=[
+            pltpu.VMEM((nodes, rows, 2 * kv_width), jnp.bfloat16),
+            pltpu.SemaphoreType.DMA((2, locals_ - 1)),
+            pltpu.SemaphoreType.DMA((2, locals_ - 1)),
+            pltpu.SemaphoreType.DMA((4, nodes // 2)),
+            pltpu.SemaphoreType.DMA((4, nodes // 2)),
+            pltpu.SemaphoreType.DMA((2,)),
+            pltpu.SemaphoreType.DMA,
+        ],
+        compiler_params=pltpu.CompilerParams(
+            collective_id=0, has_side_effects=True, vmem_limit_bytes=40 * 2**20
+        ),
+        cost_estimate=pl.CostEstimate(
+            flops=4 * seq * depth * locals_ * kv_width,
+            bytes_accessed=200 * 2**20,
+            transcendentals=0,
+        ),
+    )(tokens, key_weight, value_weight)
+
+
+def gather_kernel(
+    nodes, locals_, kg_ref, vg_ref, gain_ref, all_ref, sum_ref,
+    near, far, line_send, line_recv, node_send, node_recv, local_send, local_recv,
+):
+    node, me = lax.axis_index("node"), lax.axis_index("local")
+    kv_width = kg_ref.shape[1]
+    all_ref[me, :, :kv_width] = kg_ref[...]
+    all_ref[me, :, kv_width:] = vg_ref[...]
+    near[node] = gain_ref[...]
+    greet(nodes, locals_, node, me, True)
+    start, arrive, finish = line_gather(
+        locals_, me, all_ref.at[me], all_ref, line_send, line_recv
+    )
+    node_start, node_finish = exchange("node", nodes, node, near, node_send, node_recv)
+    local_start, local_finish = exchange("local", locals_, me, far, local_send, local_recv)
+    node_start()
+    start()
+    node_finish()
+    far[me] = jnp.sum(near[...], axis=0)
+    local_start()
+    for step in range(locals_ - 1):
+        arrive(step)
+    local_finish()
+    sum_ref[...] = jnp.sum(far[...], axis=0)
+    finish()
+
+
+def gather(nodes, locals_, key_grad, value_grad, gain_part):
+    seq, kv_width = key_grad.shape
+    vmem = pl.BlockSpec(memory_space=pltpu.VMEM)
+    return pl.pallas_call(
+        functools.partial(gather_kernel, nodes, locals_),
+        in_specs=[vmem] * 3,
+        out_specs=[vmem] * 2,
+        out_shape=[
+            jax.ShapeDtypeStruct((locals_, seq, 2 * kv_width), jnp.bfloat16),
+            jax.ShapeDtypeStruct(gain_part.shape, jnp.float32),
+        ],
+        scratch_shapes=[
+            pltpu.VMEM((nodes, *gain_part.shape), jnp.float32),
+            pltpu.VMEM((locals_, *gain_part.shape), jnp.float32),
+            pltpu.SemaphoreType.DMA((2, locals_ - 1)),
+            pltpu.SemaphoreType.DMA((2, locals_ - 1)),
+            pltpu.SemaphoreType.DMA((nodes - 1,)),
+            pltpu.SemaphoreType.DMA((nodes - 1,)),
+            pltpu.SemaphoreType.DMA((locals_ - 1,)),
+            pltpu.SemaphoreType.DMA((locals_ - 1,)),
+        ],
+        compiler_params=pltpu.CompilerParams(
+            collective_id=1, has_side_effects=True, vmem_limit_bytes=24 * 2**20
+        ),
+        cost_estimate=pl.CostEstimate(flops=0, bytes_accessed=100 * 2**20, transcendentals=0),
+    )(key_grad, value_grad, gain_part)
+
+
 def local(
-    tokens, queries, key_weight, value_weight, query_gain, key_gain, segment_ids, context_grad
+    nodes, locals_, tokens, queries, key_weight, value_weight, query_gain, key_gain, segment_ids,
+    context_grad,
 ):
     head = query_gain.shape[0]
-    kv_width = key_weight.shape[1]
+    rows, kv_width = key_weight.shape
+    ratio = nodes // locals_
     cos, sin, bias = tables(segment_ids[0], head)
     gains = jnp.stack([query_gain, key_gain], axis=1)
-    gathered = lax.all_gather(tokens, "local", axis=1, tiled=True)
-    stacked = jnp.concatenate([key_weight, value_weight], axis=1)
-    weight_all = lax.all_gather(stacked, "node", axis=0, tiled=True)
-    projected = jnp.dot(gathered, weight_all, preferred_element_type=jnp.float32)
+    gathered, projected, weight = project(nodes, locals_, tokens, key_weight, value_weight)
+    weight = weight.reshape(locals_, ratio * rows, 2 * kv_width)
     context, query_grad, key_grad, value_grad, gain_part = attention(
         queries, context_grad, projected, cos, sin, bias, gains, head
     )
-    grad_stack = jnp.concatenate([key_grad, value_grad], axis=1)
-    summed = lax.psum_scatter(
-        lax.dot_general(
-            weight_all, grad_stack, (((1,), (1,)), ((), ())), preferred_element_type=jnp.float32
-        ).astype(jnp.bfloat16),
-        "local",
-        scatter_dimension=0,
-        tiled=True,
-    )
-    token_grad = summed.T
-    weight_grad = lax.psum_scatter(
-        lax.dot_general(
-            gathered, grad_stack, (((0,), (0,)), ((), ())), preferred_element_type=jnp.float32
-        ).astype(jnp.bfloat16),
-        "node",
-        scatter_dimension=0,
-        tiled=True,
-    ).astype(jnp.float32)
-    gain_grads = lax.psum(gain_part, ("node", "local"))
+    grads = jnp.concatenate([key_grad, value_grad], axis=1)
+    weight_part = jnp.einsum("lsf,sc->lfc", gathered, grads, preferred_element_type=jnp.float32)
+    weight_part = weight_part.astype(jnp.bfloat16).reshape(nodes * rows, 2 * kv_width)
+    weight_part, gain_part = lax.optimization_barrier((weight_part, gain_part))
+    summed = lax.psum_scatter(weight_part, "node", scatter_dimension=0, tiled=True)
+    grads_all, gain_grads = gather(nodes, locals_, key_grad, value_grad, gain_part)
+    token_grad = jnp.einsum(
+        "lsc,lfc->sf", grads_all, weight, preferred_element_type=jnp.float32
+    ).astype(jnp.bfloat16)
+    weight_grad = summed.astype(jnp.float32)
     key_weight_grad = weight_grad[:, :kv_width]
     value_weight_grad = weight_grad[:, kv_width:]
     return (context, token_grad, query_grad, key_weight_grad, value_weight_grad, gain_grads)
@@ -229,4 +565,5 @@
     spread = P("node", "local")
     in_specs = (spread, spread, spread, spread, P(), P(), P("node", None), spread)
     out_specs = (spread, spread, spread, spread, spread, P())
-    return jax.shard_map(local, mesh=mesh, in_specs=in_specs, out_specs=out_specs, check_vma=False)
+    part = functools.partial(local, mesh.shape["node"], mesh.shape["local"])
+    return jax.shard_map(part, mesh=mesh, in_specs=in_specs, out_specs=out_specs, check_vma=False)

time: 355 us -> 245 us (0.69)
  waiting for transfers between devices: 242 us -> 9.99 us
  Pallas kernels: 21.3 us -> 195 us
  blocking collectives: 39.3 us -> 0 us
  matrix products: 18.4 us -> 11.2 us
    pallas_call x0 -> x2, Pallas kernels: none -> 174 us  [the longest x1 135 us: project(): pl.pallas_call(functools.partial(project_kernel, nodes, locals_), in_spec...]
    all_gather x2 -> x0, waiting for transfers between devices: 139 us -> none  [the longest x1 96.6 us: local(): gathered = lax.all_gather(tokens, 'local', axis=1, tiled=True)]
    reduce_scatter x1, waiting for transfers between devices: 92.4 us -> 9.98 us  [local(): lax.psum_scatter(weight_part, 'node', scatter_dimension=0, tiled=True)]
    psum x1 -> x0, blocking collectives: 39.3 us -> none  [local(): gain_grads = lax.psum(gain_part, ('node', 'local'))]
    unnamed x5 -> x1, waiting for transfers between devices: 11 us -> 0.02 us
    dot_general x3 -> x2, matrix products: 18.4 us -> 11.2 us  [the longest x1 6.53 us: local(): jnp.einsum('lsc,lfc->sf', grads_all, weight, preferred_element_type=jnp.f...]
    unnamed x10 -> x15, local copies, waits for them, and re-layouts: 13.9 us -> 8.47 us
  transfers between devices with their start and end apart: 4 -> 1, of which waited for: 4 -> 1; matrix products, arithmetic and copies ran while one was open for 5% -> 3% of each run, Pallas kernels for 0% -> 16%
where the time goes in v2:
time: 245 us
  Pallas kernels  195 us (80%)
  between operations  14.1 us (6%)
  matrix products  11.2 us (5%)
  local copies, waits for them, and re-layouts  11 us (4%)
  waiting for transfers between devices  9.99 us (4%)
  other arithmetic  3.5 us (1%)
    pallas_call x1, Pallas kernels, project(): pl.pallas_call(functools.partial(project_kernel, nodes, locals_), in_spec...  135 us
    pallas_call x1, Pallas kernels, gather(): pl.pallas_call(functools.partial(gather_kernel, nodes, locals_), in_specs...  38.8 us
    pallas_call x1, Pallas kernels, attention(): pl.pallas_call(functools.partial(attention_kernel, heads, block, seq // 2...  21.2 us
    reduce_scatter x1, waiting for transfers between devices, local(): lax.psum_scatter(weight_part, 'node', scatter_dimension=0, tiled=True)  9.98 us
    unnamed x15, local copies, waits for them, and re-layouts  8.47 us
    dot_general x1, matrix products, local(): jnp.einsum('lsc,lfc->sf', grads_all, weight, preferred_element_type=jnp.f...  6.53 us
  transfers between devices with their start and end apart: 1, of which 1 were waited for; matrix products, arithmetic and copies ran while one was open for 3% of the time, Pallas kernels for 16%

profile of v2, /device:TPU:0, one launch (start us, length us, event | category | flops | bytes accessed | tf_op | source)
XLA Modules:
  0.0 244.5 jit_solution(11998175217620614876)
XLA Ops:
  7.2 0.0 reduce-scatter.2.cloned.1.call-start
  7.2 0.8 compare_reduce_fusion
  8.1 0.1 add_select_fusion
  8.2 0.3 reduce-window.9
  8.5 0.1 slice.23
  8.6 0.1 slice_reduce_fusion
  8.7 0.1 fusion.5
  8.8 0.7 pad_maximum_fusion
  9.4 0.1 copy.20.gain_ref
  9.6 0.9 fusion.2.bias_ref
  10.5 0.5 multiply_sine_fusion
  11.0 0.0 copy-start.1
  11.1 1.3 copy-done.1
  12.4 0.0 copy-start.2
  12.4 1.0 copy-done.2
  13.3 0.0 copy-start.3
  13.3 1.0 copy-done.3
  14.3 0.0 copy-start
  14.3 134.7 %shard_map.127 = (bf16[4,512,1280]{2,1,0:T(8,128)(2,1)S(1)}, f32[512,512]{1,0:T(8,128)S(1)}, bf16[8,640,512]{2,1,0:T(8,128)(2,1)S(1)}) custom-call(bf16[512,1280]{1,0:T(8,128)(2,1)S(1)} %copy-done.1, bf16[640,256]{1,0:T(8,128)(2,1)S(1)} %copy-done.2, bf16[640,256]{1,0:T(8,128)(2,1)S(1)} %copy-done.3), custom_call_target="tpu_custom_call" | custom-call | flops 2684354560 | bytes 209715200 | tf_op jit(solution)/shard_map/pallas_call | solution.py:451
  149.1 0.0 copy-start.4
  149.1 2.3 copy-done.4
  151.4 0.0 copy-start.5
  151.4 2.3 copy-done.5
  153.7 0.0 copy-done
  153.7 0.0 copy-start.6
  153.7 21.2 %shard_map.128 = (bf16[512,2048]{1,0:T(8,128)(2,1)}, bf16[512,2048]{1,0:T(8,128)(2,1)}, bf16[512,256]{1,0:T(8,128)(2,1)S(1)}, bf16[512,256]{1,0:T(8,128)(2,1)S(1)}, f32[2,128]{1,0:T(2,128)S(1)}) custom-call(bf16[512,2048]{1,0:T(8,128)(2,1)S(1)} %copy-done, bf16[512,2048]{1,0:T(8,128)(2,1)} %g_ref.1, f32[512,512]{1,0:T(8,128)S(1)} %get-tuple-element.18.k_ref.v_ref, ...), custom_call_target="tpu_custom_call" | custom-call | flops 4831838208 | bytes 8388608 | tf_op jit(solution)/shard_map/pallas_call | solution.py:149
  174.9 0.0 copy-done.6
  174.9 4.7 %convolution_convert_fusion = bf16[4,1280,512]{2,1,0:T(8,128)(2,1)} fusion(bf16[4,512,1280]{2,1,0:T(8,128)(2,1)S(1)} %copy-done.6, bf16[512,256]{1,0:T(8,128)(2,1)S(1)} %get-tuple-element.21.vg_ref, bf16[512,256]{1,0:T(8,128)(2,1)S(1)} %get-tuple-element.20.kg_ref), kind=kOutput, calls=%fused_computation | convolution fusion | flops 2688024576 | bytes 11010048 | tf_op jit(solution)/shard_map/lsf,sc->lfc/dot_general | solution.py:550
  179.6 0.0 reduce-scatter.2.cloned.1.call-update
  179.6 38.8 %shard_map.129 = (bf16[4,512,512]{2,1,0:T(8,128)(2,1)S(1)}, f32[2,128]{1,0:T(2,128)S(1)}) custom-call(bf16[512,256]{1,0:T(8,128)(2,1)S(1)} %get-tuple-element.20.kg_ref, bf16[512,256]{1,0:T(8,128)(2,1)S(1)} %get-tuple-element.21.vg_ref, f32[2,128]{1,0:T(2,128)S(1)} %get-tuple-element.24.gain_ref), custom_call_target="tpu_custom_call" | custom-call | bytes 104857600 | tf_op jit(solution)/shard_map/pallas_call | solution.py:510
  218.4 6.5 %fusion = bf16[512,1280]{1,0:T(8,128)(2,1)} fusion(bf16[4,512,512]{2,1,0:T(8,128)(2,1)S(1)} %get-tuple-element.25, bf16[4,1280,512]{2,1,0:T(8,128)(2,1)} %bitcast.23), kind=kOutput, calls=%fused_computation.2 | convolution fusion | flops 2685009920 | bytes 8650752 | tf_op jit(solution)/shard_map/lsc,lfc->sf/dot_general | solution.py:555
  224.9 10.0 %reduce-scatter.2.cloned.1.call-done = bf16[640,512]{1,0:T(8,128)(2,1)} async-done(((bf16[5120,512]{1,0:T(8,128)(2,1)}), bf16[640,512]{1,0:T(8,128)(2,1)}) %reduce-scatter.2.cloned.1.call-update) | async-done | bytes 655376 | tf_op jit(solution)/shard_map/reduce_scatter | solution.py:553
  234.9 2.2 fusion.7
  237.1 0.6 copy.24
  (2 shorter events, 0.0 us)
Async XLA Ops:
  7.2 227.7 %reduce-scatter.2.cloned.1.call-start = ((), (), s32[]{:S(2)}) async-start(), calls=%async_computation.1 | async-start | bytes 5898240 | tf_op jit(solution)/shard_map/reduce_scatter | solution.py:553
  11.0 1.3 copy-start.1
  12.4 1.0 copy-start.2
  13.3 1.0 copy-start.3
  14.3 139.4 %copy-start = (bf16[512,2048]{1,0:T(8,128)(2,1)S(1)}, bf16[512,2048]{1,0:T(8,128)(2,1)}, u32[]{:S(2)}) copy-start(bf16[512,2048]{1,0:T(8,128)(2,1)} %q_ref.1) | copy-start | bytes 6291460
  149.1 2.3 copy-start.4
  151.4 2.3 copy-start.5
  153.7 21.2 %copy-start.6 = (bf16[4,512,1280]{2,1,0:T(8,128)(2,1)S(1)}, bf16[4,512,1280]{2,1,0:T(8,128)(2,1)}, u32[]{:S(2)}) copy-start(bf16[4,512,1280]{2,1,0:T(8,128)(2,1)} %copy-done.5) | copy-start | bytes 15728644
Sparse Core Ops, SparseCore 0:
  179.7 55.1 reduce-scatter.1
